TPU v7x, 32 devices: a whole 2x2x4 slice. The times are simulated.
32 devices in a mesh: view: 2 (over y), batch: 16 (over z, x, core).
Axes of the slice: x: 2, y: 2, z: 4, core: 2. Of those that a mesh axis runs over, the one named last changes fastest.
Arguments:
- embeddings: bfloat16 [2, 2048, 256], P('view', 'batch'), may hold values from -1.5 to 1.5
- positive: int32 [2, 2048], P(None, 'batch'), may hold values from 0 to 127, as said below
Outputs:
- gradients: float32 [2, 2048, 256], P('view', 'batch')
- totals: float32 [2, 2048], P('view', 'batch')
- row_loss: float32 [2, 2048], P('view', 'batch')
Inputs may be any that keep to these rules, and one draw needn't show every extreme that they name: `positive`: for each view and each aligned block of 128 samples, the entries are a permutation of 0 to 127.
All inputs are finite; a program needn't handle non-finite values.
Results may differ from a plain program's by a relative error of at most 0.002.
Values may be sent and summed in bfloat16 or wider, within the bound.
A program may use at most 64 MiB of HBM per device.

v0:
```python
import jax
import jax.numpy as jnp
from jax import lax
from jax.sharding import PartitionSpec as P

logit_scale = 10.0


def from_partner(value, axis, bit):
    return lax.ppermute(value, axis, [(i, i ^ 1 << bit) for i in range(lax.axis_size(axis))])


def merge_stats(first_stats, second_stats):
    top_value = jnp.maximum(first_stats[0], second_stats[0])
    summed = first_stats[1] * jnp.exp(first_stats[0] - top_value) + second_stats[1] * jnp.exp(
        second_stats[0] - top_value
    )
    return (top_value, summed)


def bit_set(batch_index, bit_pos):
    return jnp.bitwise_and(jnp.right_shift(batch_index, bit_pos), 1) == 1


def tile_terms(own_rows, partner, is_key, swap_bit):
    row_count = own_rows.shape[0]
    embed_width = own_rows.shape[1]
    batch_bits = lax.axis_size("batch").bit_length() - 1
    col_bits = batch_bits // 2
    row_bits = batch_bits - 1 - col_bits
    top_bit = batch_bits - 1
    batch_index = lax.axis_index("batch")
    flipped = from_partner(partner, "batch", top_bit)
    row_tile = jnp.where(is_key, flipped, own_rows)
    col_tile = jnp.where(is_key, own_rows, partner)
    for bit_pos in range(row_bits):
        other_half = from_partner(row_tile, "batch", bit_pos)
        row_tile = jnp.where(
            bit_set(batch_index, bit_pos),
            jnp.concatenate([other_half, row_tile], axis=0),
            jnp.concatenate([row_tile, other_half], axis=0),
        )
    for bit_pos in range(row_bits, row_bits + col_bits):
        other_half = from_partner(col_tile, "batch", bit_pos)
        col_tile = jnp.where(
            bit_set(batch_index, bit_pos),
            jnp.concatenate([other_half, col_tile], axis=0),
            jnp.concatenate([col_tile, other_half], axis=0),
        )
    col_blocks = col_tile.reshape(2**col_bits, row_count, embed_width)
    tile_rows = row_tile.shape[0]

    def tile_scores(key_piece):
        return (
            jnp.einsum("ie,je->ij", row_tile, key_piece, preferred_element_type=jnp.float32)
            * logit_scale
        )

    def stat_step(running, key_piece):
        scores = tile_scores(key_piece)
        column_max = jnp.max(scores, axis=0)
        column_sum = jnp.sum(jnp.exp(scores - column_max[None, :]), axis=0)
        block_max = jnp.max(scores, axis=1)
        block_sum = jnp.sum(jnp.exp(scores - block_max[:, None]), axis=1)
        return (merge_stats(running, (block_max, block_sum)), (column_max, column_sum))

    start_state = (jnp.full((tile_rows,), -1e30, jnp.float32), jnp.zeros((tile_rows,), jnp.float32))
    row_state, col_state = lax.scan(stat_step, start_state, col_blocks)
    for bit_pos in range(row_bits):
        far_state = from_partner((row_state[0], row_state[1]), "batch", bit_pos)
        row_state = merge_stats(row_state, far_state)
    for bit_pos in range(row_bits, row_bits + col_bits):
        far_state = from_partner((col_state[0], col_state[1]), "batch", bit_pos)
        col_state = merge_stats(col_state, far_state)
    across = from_partner(
        (row_state[0], row_state[1], col_state[0], col_state[1]), "view", swap_bit
    )
    col_state = merge_stats(col_state, (across[2], across[3]))
    row_far = from_partner((across[0], across[1]), "batch", top_bit)
    row_state = merge_stats(row_state, row_far)
    row_total = row_state[0] + jnp.log(row_state[1])
    col_total = col_state[0] + jnp.log(col_state[1])

    def grad_tile_step(row_acc, scan_entry):
        key_piece, column_total = scan_entry
        scores = tile_scores(key_piece)
        w_rows = jnp.exp(scores - row_total[:, None]).astype(jnp.bfloat16)
        w_cols = jnp.exp(scores - column_total[None, :]).astype(jnp.bfloat16)
        row_acc = (
            row_acc
            + jnp.dot(w_rows, key_piece, preferred_element_type=jnp.float32)
            + jnp.dot(w_cols, key_piece, preferred_element_type=jnp.float32)
        )
        col_part = jnp.einsum(
            "ij,ie->je", w_cols, row_tile, preferred_element_type=jnp.float32
        ) + jnp.einsum("ij,ie->je", w_rows, row_tile, preferred_element_type=jnp.float32)
        return (row_acc, col_part)

    row_acc, col_parts = lax.scan(
        grad_tile_step, jnp.zeros((tile_rows, embed_width), jnp.float32), (col_blocks, col_total)
    )
    col_acc = col_parts.reshape(-1, embed_width)
    for bit_pos in reversed(range(row_bits)):
        half_rows = row_acc.shape[0] // 2
        mine_upper = bit_set(batch_index, bit_pos)
        kept_half = jnp.where(mine_upper, row_acc[half_rows:], row_acc[:half_rows])
        sent_half = jnp.where(mine_upper, row_acc[:half_rows], row_acc[half_rows:])
        row_acc = kept_half + from_partner(sent_half, "batch", bit_pos)
    for bit_pos in reversed(range(row_bits, row_bits + col_bits)):
        half_rows = col_acc.shape[0] // 2
        mine_upper = bit_set(batch_index, bit_pos)
        kept_half = jnp.where(mine_upper, col_acc[half_rows:], col_acc[:half_rows])
        sent_half = jnp.where(mine_upper, col_acc[:half_rows], col_acc[half_rows:])
        col_acc = kept_half + from_partner(sent_half, "batch", bit_pos)
    payload = jnp.where(is_key, row_acc, col_acc)
    returned = from_partner(payload, "view", swap_bit)
    relayed = from_partner(returned, "batch", top_bit)
    spread = jnp.where(is_key, col_acc + returned, row_acc + relayed)
    low_index = jnp.bitwise_and(batch_index, 2**row_bits - 1)
    mid_index = jnp.bitwise_and(jnp.right_shift(batch_index, row_bits), 2**col_bits - 1)
    anchor_total = lax.dynamic_slice_in_dim(row_total, low_index * row_count, row_count, 0)
    key_total = lax.dynamic_index_in_dim(col_total, mid_index, 0, keepdims=False)
    totals = jnp.where(is_key, key_total, anchor_total)
    return (totals, spread)


def body(embeddings, positive):
    own_rows = embeddings[0]
    row_count = own_rows.shape[0]
    view_count = lax.axis_size("view")
    swap_bit = view_count.bit_length() - 2
    partner = from_partner(own_rows, "view", swap_bit)
    view_index = lax.axis_index("view")
    is_key = view_index // (view_count // 2) == 1
    own_match = lax.dynamic_index_in_dim(positive, view_index, 0, keepdims=False)
    far_match = lax.dynamic_index_in_dim(
        positive, jnp.bitwise_xor(view_index, view_count // 2), 0, keepdims=False
    )
    totals, spread = tile_terms(own_rows, partner, is_key, swap_bit)
    pos_rows = jnp.take(partner, own_match, axis=0).astype(jnp.float32)
    pos_score = jnp.sum(own_rows.astype(jnp.float32) * pos_rows, axis=1) * logit_scale
    row_loss = totals - pos_score
    row_ids = jnp.arange(row_count, dtype=jnp.int32)
    matched_hot = (far_match[None, :] == row_ids[:, None]).astype(jnp.bfloat16)
    matched = jnp.dot(matched_hot, partner, preferred_element_type=jnp.float32)
    gradients = logit_scale * (spread - pos_rows - matched)
    return (gradients[None], totals[None], row_loss[None])


def solution(mesh):
    return jax.shard_map(
        body,
        mesh=mesh,
        in_specs=(P("view", "batch", None), P(None, "batch")),
        out_specs=(P("view", "batch", None), P("view", "batch"), P("view", "batch")),
        check_vma=False,
    )
```

profile of v0, /device:TPU:0, one launch (start us, length us, event | category | flops | bytes accessed | tf_op | source)
XLA Modules:
  0.0 71.9 jit_solution(13202746135795656125)
XLA Ops:
  0.6 3.0 %collective-permute-start = (bf16[128,256]{1,0:T(8,128)(2,1)}, bf16[128,256]{1,0:T(8,128)(2,1)S(1)}, u32[]{:S(2)}, u32[]{:S(2)}) collective-permute-start(bf16[128,256]{1,0:T(8,128)(2,1)} %bitcast.76), channel_id=1, source_target_pairs={{0,16},{16,0},{1,17},{17,1},{2,18},{18,2},{3,19},{19,3},{4,20},{20... | collective-permute-start | bytes 196616 | tf_op jit(solution)/shard_map/ppermute | solution.py:10
  3.7 2.5 %collective-permute-done = bf16[128,256]{1,0:T(8,128)(2,1)S(1)} collective-permute-done((bf16[128,256]{1,0:T(8,128)(2,1)}, bf16[128,256]{1,0:T(8,128)(2,1)S(1)}, u32[]{:S(2)}, u32[]{:S(2)}) %collective-permute-start) | collective-permute-done | bytes 65568 | tf_op jit(solution)/shard_map/ppermute | solution.py:10
  6.1 3.1 %collective-permute-start.3 = (bf16[128,256]{1,0:T(8,128)(2,1)S(1)}, bf16[128,256]{1,0:T(8,128)(2,1)S(1)}, u32[]{:S(2)}, u32[]{:S(2)}) collective-permute-start(bf16[128,256]{1,0:T(8,128)(2,1)S(1)} %collective-permute-done), channel_id=1, source_target_pairs={{0,8},{1,9},{2,10},{3,11},{4,12},{5,13},{6,14},{7,15},{8,0},{9,1},... | collective-permute-start | bytes 196616 | tf_op jit(solution)/shard_map/ppermute | solution.py:10
  9.2 2.2 %collective-permute-done.3 = bf16[128,256]{1,0:T(8,128)(2,1)S(1)} collective-permute-done((bf16[128,256]{1,0:T(8,128)(2,1)S(1)}, bf16[128,256]{1,0:T(8,128)(2,1)S(1)}, u32[]{:S(2)}, u32[]{:S(2)}) %collective-permute-start.3) | collective-permute-done | bytes 65568 | tf_op jit(solution)/shard_map/ppermute | solution.py:10
  11.5 0.9 %broadcast_select_fusion.3 = (bf16[128,256]{1,0:T(8,128)(2,1)S(1)}, bf16[128,256]{1,0:T(8,128)(2,1)S(1)}) fusion(bf16[128,256]{1,0:T(8,128)(2,1)S(1)} %collective-permute-done.3, pred[]{:T(512)S(6)} %eq.30, bf16[1,128,256]{2,1,0:T(8,128)(2,1)} %param.6, bf16[128,256]{1,0:T(8,128)(2,1)S(1)} %collective-permute-done), kind=kLoop, calls=%fused_computation.51 | loop fusion | flops 65536 | bytes 327681 | tf_op jit(solution)/shard_map/jit(_where)/select_n | solution.py:34
  12.3 1.9 %collective-permute-start.1 = (bf16[128,256]{1,0:T(8,128)(2,1)S(1)}, bf16[128,256]{1,0:T(8,128)(2,1)S(1)}, u32[]{:S(2)}, u32[]{:S(2)}) collective-permute-start(bf16[128,256]{1,0:T(8,128)(2,1)S(1)} %get-tuple-element.184), channel_id=1, source_target_pairs={{0,2},{1,3},{2,0},{3,1},{4,6},{5,7},{6,4},{7,5},{8,10},{9,11},{10,... | collective-permute-start | bytes 196616 | tf_op jit(solution)/shard_map/ppermute | solution.py:10
  14.2 2.4 %collective-permute-done.1 = bf16[128,256]{1,0:T(8,128)(2,1)S(1)} collective-permute-done((bf16[128,256]{1,0:T(8,128)(2,1)S(1)}, bf16[128,256]{1,0:T(8,128)(2,1)S(1)}, u32[]{:S(2)}, u32[]{:S(2)}) %collective-permute-start.1) | collective-permute-done | bytes 65568 | tf_op jit(solution)/shard_map/ppermute | solution.py:10
  16.7 2.0 %collective-permute-start.2 = (bf16[256,256]{1,0:T(8,128)(2,1)S(1)}, bf16[256,256]{1,0:T(8,128)(2,1)S(1)}, u32[]{:S(2)}, u32[]{:S(2)}) collective-permute-start(bf16[256,256]{1,0:T(8,128)(2,1)S(1)} %maximum_select_fusion.1), channel_id=1, source_target_pairs={{0,4},{1,5},{2,6},{3,7},{4,0},{5,1},{6,2},{7,3},{8,12},{9,13},{10,... | collective-permute-start | bytes 393224 | tf_op jit(solution)/shard_map/ppermute | solution.py:10
  18.7 3.0 %collective-permute-done.2 = bf16[256,256]{1,0:T(8,128)(2,1)S(1)} collective-permute-done((bf16[256,256]{1,0:T(8,128)(2,1)S(1)}, bf16[256,256]{1,0:T(8,128)(2,1)S(1)}, u32[]{:S(2)}, u32[]{:S(2)}) %collective-permute-start.2) | collective-permute-done | bytes 131104 | tf_op jit(solution)/shard_map/ppermute | solution.py:10
  21.8 2.4 %while.30 = (s32[]{:T(128)}, f32[256]{0:T(256)S(1)}, f32[256]{0:T(256)S(1)}, f32[4,128]{1,0:T(4,128)S(1)}, f32[4,128]{1,0:T(4,128)S(1)}, /*index=5*/bf16[4,128,2...) while((s32[]{:T(128)}, f32[256]{0:T(256)S(1)}, f32[256]{0:T(256)S(1)}, ...), condition=%wide.region_5.6_spmd.clone, body=%wide.region_0.5_spmd.clone.sunk | while | flops 17007872 | bytes 471667 | solution.py:68
  24.2 1.9 %collective-permute-start.11 = (f32[4,128]{1,0:T(4,128)S(1)}, f32[4,128]{1,0:T(4,128)S(1)}, u32[]{:S(2)}, u32[]{:S(2)}) collective-permute-start(f32[4,128]{1,0:T(4,128)S(1)} %get-tuple-element.83), channel_id=1, source_target_pairs={{0,2},{1,3},{2,0},{3,1},{4,6},{5,7},{6,4},{7,5},{8,10},{9,11},{10,... | collective-permute-start | bytes 6152 | tf_op jit(solution)/shard_map/ppermute | solution.py:10
  26.8 1.0 %collective-permute-done.11 = f32[4,128]{1,0:T(4,128)S(1)} collective-permute-done((f32[4,128]{1,0:T(4,128)S(1)}, f32[4,128]{1,0:T(4,128)S(1)}, u32[]{:S(2)}, u32[]{:S(2)}) %collective-permute-start.11) | collective-permute-done | bytes 2080 | tf_op jit(solution)/shard_map/ppermute | solution.py:10
  27.8 1.8 %collective-permute-done.14 = f32[4,128]{1,0:T(4,128)S(1)} collective-permute-done((f32[4,128]{1,0:T(4,128)S(1)}, f32[4,128]{1,0:T(4,128)S(1)}, u32[]{:S(2)}, u32[]{:S(2)}) %collective-permute-start.14) | collective-permute-done | bytes 2080 | tf_op jit(solution)/shard_map/ppermute | solution.py:10
  29.7 1.6 %collective-permute-start.12 = (f32[4,128]{1,0:T(4,128)S(1)}, f32[4,128]{1,0:T(4,128)S(1)}, u32[]{:S(2)}, u32[]{:S(2)}) collective-permute-start(f32[4,128]{1,0:T(4,128)S(1)} %get-tuple-element.177), channel_id=1, source_target_pairs={{0,4},{1,5},{2,6},{3,7},{4,0},{5,1},{6,2},{7,3},{8,12},{9,13},{10,... | collective-permute-start | bytes 6152 | tf_op jit(solution)/shard_map/ppermute | solution.py:10
  31.8 1.6 %collective-permute-start.9 = (f32[256]{0:T(256)S(1)}, f32[256]{0:T(256)S(1)}, u32[]{:S(2)}, u32[]{:S(2)}) collective-permute-start(f32[256]{0:T(256)S(1)} %get-tuple-element.178), channel_id=1, source_target_pairs={{0,16},{16,0},{1,17},{17,1},{2,18},{18,2},{3,19},{19,3},{4,20},{20... | collective-permute-start | bytes 3080 | tf_op jit(solution)/shard_map/ppermute | solution.py:10
  33.9 1.5 %collective-permute-done.9 = f32[256]{0:T(256)S(1)} collective-permute-done((f32[256]{0:T(256)S(1)}, f32[256]{0:T(256)S(1)}, u32[]{:S(2)}, u32[]{:S(2)}) %collective-permute-start.9) | collective-permute-done | bytes 1056 | tf_op jit(solution)/shard_map/ppermute | solution.py:10
  35.4 2.8 %collective-permute-start.10 = (f32[256]{0:T(256)S(1)}, f32[256]{0:T(256)S(1)}, u32[]{:S(2)}, u32[]{:S(2)}) collective-permute-start(f32[256]{0:T(256)S(1)} %collective-permute-done.9), channel_id=1, source_target_pairs={{0,8},{1,9},{2,10},{3,11},{4,12},{5,13},{6,14},{7,15},{8,0},{9,1},... | collective-permute-start | bytes 3080 | tf_op jit(solution)/shard_map/ppermute | solution.py:10
  38.2 1.5 %collective-permute-start.7 = (f32[256]{0:T(256)S(1)}, f32[256]{0:T(256)S(1)}, u32[]{:S(2)}, u32[]{:S(2)}) collective-permute-start(f32[256]{0:T(256)S(1)} %collective-permute-done.6), channel_id=1, source_target_pairs={{0,8},{1,9},{2,10},{3,11},{4,12},{5,13},{6,14},{7,15},{8,0},{9,1},... | collective-permute-start | bytes 3080 | tf_op jit(solution)/shard_map/ppermute | solution.py:10
  40.3 1.5 %collective-permute-start.16 = (f32[4,128]{1,0:T(4,128)S(1)}, f32[4,128]{1,0:T(4,128)S(1)}, u32[]{:S(2)}, u32[]{:S(2)}) collective-permute-start(f32[4,128]{1,0:T(4,128)S(1)} %get-tuple-element.174), channel_id=1, source_target_pairs={{0,16},{16,0},{1,17},{17,1},{2,18},{18,2},{3,19},{19,3},{4,20},{20... | collective-permute-start | bytes 6152 | tf_op jit(solution)/shard_map/ppermute | solution.py:10
  41.9 0.8 %collective-permute-done.7 = f32[256]{0:T(256)S(1)} collective-permute-done((f32[256]{0:T(256)S(1)}, f32[256]{0:T(256)S(1)}, u32[]{:S(2)}, u32[]{:S(2)}) %collective-permute-start.7) | collective-permute-done | bytes 1056 | tf_op jit(solution)/shard_map/ppermute | solution.py:10
  42.7 0.7 collective-permute-done.13
  43.9 4.6 %while.31 = (s32[]{:T(128)}, f32[256,256]{1,0:T(8,128)S(1)}, f32[4,128,256]{2,1,0:T(8,128)S(1)}, bf16[4,128,256]{2,1,0:T(8,128)(2,1)S(1)}, bf16[256,256]{1,0:T(8...) while((s32[]{:T(128)}, f32[256,256]{1,0:T(8,128)S(1)}, ...), condition=%wide.region_7.8_spmd.clone, body=%wide.region_6.7_spmd.clone.sunk | while | flops 84410368 | bytes 2691195 | solution.py:99
  48.6 2.0 %collective-permute-start.17 = (f32[256,256]{1,0:T(8,128)S(1)}, f32[256,256]{1,0:T(8,128)S(1)}, u32[]{:S(2)}, u32[]{:S(2)}) collective-permute-start(f32[256,256]{1,0:T(8,128)S(1)} %bitcast.77), channel_id=1, source_target_pairs={{0,4},{1,5},{2,6},{3,7},{4,0},{5,1},{6,2},{7,3},{8,12},{9,13},{10,... | collective-permute-start | bytes 786440 | tf_op jit(solution)/shard_map/ppermute | solution.py:10
  50.7 4.3 %collective-permute-done.17 = f32[256,256]{1,0:T(8,128)S(1)} collective-permute-done((f32[256,256]{1,0:T(8,128)S(1)}, f32[256,256]{1,0:T(8,128)S(1)}, u32[]{:S(2)}, u32[]{:S(2)}) %collective-permute-start.17) | collective-permute-done | bytes 262176 | tf_op jit(solution)/shard_map/ppermute | solution.py:10
  55.1 0.6 collective-permute-start.18
  55.8 4.4 %collective-permute-done.18 = f32[128,256]{1,0:T(8,128)S(1)} collective-permute-done((f32[128,256]{1,0:T(8,128)S(1)}, f32[128,256]{1,0:T(8,128)S(1)}, u32[]{:S(2)}, u32[]{:S(2)}) %collective-permute-start.18) | collective-permute-done | bytes 131104 | tf_op jit(solution)/shard_map/ppermute | solution.py:10
  60.2 1.6 %collective-permute-start.20 = (f32[128,256]{1,0:T(8,128)S(1)}, f32[128,256]{1,0:T(8,128)S(1)}, u32[]{:S(2)}, u32[]{:S(2)}) collective-permute-start(f32[128,256]{1,0:T(8,128)S(1)} %get-tuple-element.171), channel_id=1, source_target_pairs={{0,16},{16,0},{1,17},{17,1},{2,18},{18,2},{3,19},{19,3},{4,20},{20... | collective-permute-start | bytes 393224 | tf_op jit(solution)/shard_map/ppermute | solution.py:10
  61.8 0.8 %gather_fusion = bf16[128,256]{1,0:T(8,128)(2,1)S(1)} fusion(bf16[128,256]{1,0:T(8,128)(2,1)S(1)} %collective-permute-done, s32[1024]{0:T(1024)S(1)} %pad_clamp_fusion), kind=kCustom, calls=%fused_computation | custom fusion | bytes 131584 | tf_op jit(solution)/shard_map/jit(_take)/gather | solution.py:140
  62.8 2.4 %collective-permute-done.20 = f32[128,256]{1,0:T(8,128)S(1)} collective-permute-done((f32[128,256]{1,0:T(8,128)S(1)}, f32[128,256]{1,0:T(8,128)S(1)}, u32[]{:S(2)}, u32[]{:S(2)}) %collective-permute-start.20) | collective-permute-done | bytes 131104 | tf_op jit(solution)/shard_map/ppermute | solution.py:10
  65.2 2.4 %collective-permute-start.21 = (f32[128,256]{1,0:T(8,128)S(1)}, f32[128,256]{1,0:T(8,128)S(1)}, u32[]{:S(2)}, u32[]{:S(2)}) collective-permute-start(f32[128,256]{1,0:T(8,128)S(1)} %collective-permute-done.20), channel_id=1, source_target_pairs={{0,8},{1,9},{2,10},{3,11},{4,12},{5,13},{6,14},{7,15},{8,0},{9,1},... | collective-permute-start | bytes 393224 | tf_op jit(solution)/shard_map/ppermute | solution.py:10
  68.3 2.9 %collective-permute-done.21 = f32[128,256]{1,0:T(8,128)S(1)} collective-permute-done((f32[128,256]{1,0:T(8,128)S(1)}, f32[128,256]{1,0:T(8,128)S(1)}, u32[]{:S(2)}, u32[]{:S(2)}) %collective-permute-start.21) | collective-permute-done | bytes 131104 | tf_op jit(solution)/shard_map/ppermute | solution.py:10
  71.1 0.8 %fusion.20 = f32[1,128,256]{2,1,0:T(8,128)} fusion(f32[128,256]{1,0:T(8,128)S(1)} %get-tuple-element.173, f32[128,256]{1,0:T(8,128)S(1)} %collective-permute-done.21, f32[128,256]{1,0:T(8,128)S(1)} %get-tuple-element.172, f32[128,256]{1,0:T(8,128)S(1)} %collective-permute-done.20, bf16[128,256]{1,0:T(8,128)(2,1)S(1)} %collective-permute-done, pred[]{:T(512)S(6)} %eq.30, ...), kind=kOutput, calls=%fused_computation.39 | convolution fusion | flops 8667136 | bytes 787073 | tf_op jit(solution)/shard_map/dot_general | solution.py:145
  (90 shorter events, 10.7 us)
Async XLA Ops:
  0.6 5.5 %collective-permute-start = (bf16[128,256]{1,0:T(8,128)(2,1)}, bf16[128,256]{1,0:T(8,128)(2,1)S(1)}, u32[]{:S(2)}, u32[]{:S(2)}) collective-permute-start(bf16[128,256]{1,0:T(8,128)(2,1)} %bitcast.76), channel_id=1, source_target_pairs={{0,16},{16,0},{1,17},{17,1},{2,18},{18,2},{3,19},{19,3},{4,20},{20... | collective-permute-start | bytes 196616 | tf_op jit(solution)/shard_map/ppermute | solution.py:10
  6.1 5.3 %collective-permute-start.3 = (bf16[128,256]{1,0:T(8,128)(2,1)S(1)}, bf16[128,256]{1,0:T(8,128)(2,1)S(1)}, u32[]{:S(2)}, u32[]{:S(2)}) collective-permute-start(bf16[128,256]{1,0:T(8,128)(2,1)S(1)} %collective-permute-done), channel_id=1, source_target_pairs={{0,8},{1,9},{2,10},{3,11},{4,12},{5,13},{6,14},{7,15},{8,0},{9,1},... | collective-permute-start | bytes 196616 | tf_op jit(solution)/shard_map/ppermute | solution.py:10
  12.3 4.3 %collective-permute-start.1 = (bf16[128,256]{1,0:T(8,128)(2,1)S(1)}, bf16[128,256]{1,0:T(8,128)(2,1)S(1)}, u32[]{:S(2)}, u32[]{:S(2)}) collective-permute-start(bf16[128,256]{1,0:T(8,128)(2,1)S(1)} %get-tuple-element.184), channel_id=1, source_target_pairs={{0,2},{1,3},{2,0},{3,1},{4,6},{5,7},{6,4},{7,5},{8,10},{9,11},{10,... | collective-permute-start | bytes 196616 | tf_op jit(solution)/shard_map/ppermute | solution.py:10
  14.2 4.5 %collective-permute-start.4 = (bf16[128,256]{1,0:T(8,128)(2,1)S(1)}, bf16[128,256]{1,0:T(8,128)(2,1)S(1)}, u32[]{:S(2)}, u32[]{:S(2)}) collective-permute-start(bf16[128,256]{1,0:T(8,128)(2,1)S(1)} %get-tuple-element.183), channel_id=1, source_target_pairs={{0,1},{1,0},{2,3},{3,2},{4,5},{5,4},{6,7},{7,6},{8,9},{9,8},{10,11... | collective-permute-start | bytes 196616 | tf_op jit(solution)/shard_map/ppermute | solution.py:10
  16.7 5.0 %collective-permute-start.2 = (bf16[256,256]{1,0:T(8,128)(2,1)S(1)}, bf16[256,256]{1,0:T(8,128)(2,1)S(1)}, u32[]{:S(2)}, u32[]{:S(2)}) collective-permute-start(bf16[256,256]{1,0:T(8,128)(2,1)S(1)} %maximum_select_fusion.1), channel_id=1, source_target_pairs={{0,4},{1,5},{2,6},{3,7},{4,0},{5,1},{6,2},{7,3},{8,12},{9,13},{10,... | collective-permute-start | bytes 393224 | tf_op jit(solution)/shard_map/ppermute | solution.py:10
  24.2 3.6 %collective-permute-start.11 = (f32[4,128]{1,0:T(4,128)S(1)}, f32[4,128]{1,0:T(4,128)S(1)}, u32[]{:S(2)}, u32[]{:S(2)}) collective-permute-start(f32[4,128]{1,0:T(4,128)S(1)} %get-tuple-element.83), channel_id=1, source_target_pairs={{0,2},{1,3},{2,0},{3,1},{4,6},{5,7},{6,4},{7,5},{8,10},{9,11},{10,... | collective-permute-start | bytes 6152 | tf_op jit(solution)/shard_map/ppermute | solution.py:10
  26.1 3.6 %collective-permute-start.14 = (f32[4,128]{1,0:T(4,128)S(1)}, f32[4,128]{1,0:T(4,128)S(1)}, u32[]{:S(2)}, u32[]{:S(2)}) collective-permute-start(f32[4,128]{1,0:T(4,128)S(1)} %get-tuple-element.84), channel_id=1, source_target_pairs={{0,2},{1,3},{2,0},{3,1},{4,6},{5,7},{6,4},{7,5},{8,10},{9,11},{10,... | collective-permute-start | bytes 6152 | tf_op jit(solution)/shard_map/ppermute | solution.py:10
  26.3 5.5 %collective-permute-start.5 = (f32[256]{0:T(256)S(1)}, f32[256]{0:T(256)S(1)}, u32[]{:S(2)}, u32[]{:S(2)}) collective-permute-start(f32[256]{0:T(256)S(1)} %get-tuple-element.81), channel_id=1, source_target_pairs={{0,1},{1,0},{2,3},{3,2},{4,5},{5,4},{6,7},{7,6},{8,9},{9,8},{10,11... | collective-permute-start | bytes 3080 | tf_op jit(solution)/shard_map/ppermute | solution.py:10
  26.3 5.5 %collective-permute-start.8 = (f32[256]{0:T(256)S(1)}, f32[256]{0:T(256)S(1)}, u32[]{:S(2)}, u32[]{:S(2)}) collective-permute-start(f32[256]{0:T(256)S(1)} %get-tuple-element.82), channel_id=1, source_target_pairs={{0,1},{1,0},{2,3},{3,2},{4,5},{5,4},{6,7},{7,6},{8,9},{9,8},{10,11... | collective-permute-start | bytes 3080 | tf_op jit(solution)/shard_map/ppermute | solution.py:10
  29.7 10.1 %collective-permute-start.12 = (f32[4,128]{1,0:T(4,128)S(1)}, f32[4,128]{1,0:T(4,128)S(1)}, u32[]{:S(2)}, u32[]{:S(2)}) collective-permute-start(f32[4,128]{1,0:T(4,128)S(1)} %get-tuple-element.177), channel_id=1, source_target_pairs={{0,4},{1,5},{2,6},{3,7},{4,0},{5,1},{6,2},{7,3},{8,12},{9,13},{10,... | collective-permute-start | bytes 6152 | tf_op jit(solution)/shard_map/ppermute | solution.py:10
  31.3 8.4 %collective-permute-start.15 = (f32[4,128]{1,0:T(4,128)S(1)}, f32[4,128]{1,0:T(4,128)S(1)}, u32[]{:S(2)}, u32[]{:S(2)}) collective-permute-start(f32[4,128]{1,0:T(4,128)S(1)} %get-tuple-element.176), channel_id=1, source_target_pairs={{0,4},{1,5},{2,6},{3,7},{4,0},{5,1},{6,2},{7,3},{8,12},{9,13},{10,... | collective-permute-start | bytes 6152 | tf_op jit(solution)/shard_map/ppermute | solution.py:10
  31.8 3.6 %collective-permute-start.9 = (f32[256]{0:T(256)S(1)}, f32[256]{0:T(256)S(1)}, u32[]{:S(2)}, u32[]{:S(2)}) collective-permute-start(f32[256]{0:T(256)S(1)} %get-tuple-element.178), channel_id=1, source_target_pairs={{0,16},{16,0},{1,17},{17,1},{2,18},{18,2},{3,19},{19,3},{4,20},{20... | collective-permute-start | bytes 3080 | tf_op jit(solution)/shard_map/ppermute | solution.py:10
  33.4 4.9 %collective-permute-start.6 = (f32[256]{0:T(256)S(1)}, f32[256]{0:T(256)S(1)}, u32[]{:S(2)}, u32[]{:S(2)}) collective-permute-start(f32[256]{0:T(256)S(1)} %get-tuple-element.179), channel_id=1, source_target_pairs={{0,16},{16,0},{1,17},{17,1},{2,18},{18,2},{3,19},{19,3},{4,20},{20... | collective-permute-start | bytes 3080 | tf_op jit(solution)/shard_map/ppermute | solution.py:10
  35.4 6.4 %collective-permute-start.10 = (f32[256]{0:T(256)S(1)}, f32[256]{0:T(256)S(1)}, u32[]{:S(2)}, u32[]{:S(2)}) collective-permute-start(f32[256]{0:T(256)S(1)} %collective-permute-done.9), channel_id=1, source_target_pairs={{0,8},{1,9},{2,10},{3,11},{4,12},{5,13},{6,14},{7,15},{8,0},{9,1},... | collective-permute-start | bytes 3080 | tf_op jit(solution)/shard_map/ppermute | solution.py:10
  38.2 4.5 %collective-permute-start.7 = (f32[256]{0:T(256)S(1)}, f32[256]{0:T(256)S(1)}, u32[]{:S(2)}, u32[]{:S(2)}) collective-permute-start(f32[256]{0:T(256)S(1)} %collective-permute-done.6), channel_id=1, source_target_pairs={{0,8},{1,9},{2,10},{3,11},{4,12},{5,13},{6,14},{7,15},{8,0},{9,1},... | collective-permute-start | bytes 3080 | tf_op jit(solution)/shard_map/ppermute | solution.py:10
  39.8 3.7 %collective-permute-start.13 = (f32[4,128]{1,0:T(4,128)S(1)}, f32[4,128]{1,0:T(4,128)S(1)}, u32[]{:S(2)}, u32[]{:S(2)}) collective-permute-start(f32[4,128]{1,0:T(4,128)S(1)} %get-tuple-element.175), channel_id=1, source_target_pairs={{0,16},{16,0},{1,17},{17,1},{2,18},{18,2},{3,19},{19,3},{4,20},{20... | collective-permute-start | bytes 6152 | tf_op jit(solution)/shard_map/ppermute | solution.py:10
  40.3 3.6 %collective-permute-start.16 = (f32[4,128]{1,0:T(4,128)S(1)}, f32[4,128]{1,0:T(4,128)S(1)}, u32[]{:S(2)}, u32[]{:S(2)}) collective-permute-start(f32[4,128]{1,0:T(4,128)S(1)} %get-tuple-element.174), channel_id=1, source_target_pairs={{0,16},{16,0},{1,17},{17,1},{2,18},{18,2},{3,19},{19,3},{4,20},{20... | collective-permute-start | bytes 6152 | tf_op jit(solution)/shard_map/ppermute | solution.py:10
  48.6 2.0 %copy-start.1 = (s32[2,128]{1,0:T(2,128)S(1)}, s32[2,128]{1,0:T(2,128)}, u32[]{:S(2)}) copy-start(s32[2,128]{1,0:T(2,128)} %param.7) | copy-start | bytes 3076
  48.6 6.4 %collective-permute-start.17 = (f32[256,256]{1,0:T(8,128)S(1)}, f32[256,256]{1,0:T(8,128)S(1)}, u32[]{:S(2)}, u32[]{:S(2)}) collective-permute-start(f32[256,256]{1,0:T(8,128)S(1)} %bitcast.77), channel_id=1, source_target_pairs={{0,4},{1,5},{2,6},{3,7},{4,0},{5,1},{6,2},{7,3},{8,12},{9,13},{10,... | collective-permute-start | bytes 786440 | tf_op jit(solution)/shard_map/ppermute | solution.py:10
  50.7 5.1 %collective-permute-start.19 = (f32[128,256]{1,0:T(8,128)S(1)}, f32[128,256]{1,0:T(8,128)S(1)}, u32[]{:S(2)}, u32[]{:S(2)}) collective-permute-start(f32[128,256]{1,0:T(8,128)S(1)} %slice_select_fusion.3), channel_id=1, source_target_pairs={{0,1},{1,0},{2,3},{3,2},{4,5},{5,4},{6,7},{7,6},{8,9},{9,8},{10,11... | collective-permute-start | bytes 393224 | tf_op jit(solution)/shard_map/ppermute | solution.py:10
  55.1 5.0 %collective-permute-start.18 = (f32[128,256]{1,0:T(8,128)S(1)}, f32[128,256]{1,0:T(8,128)S(1)}, u32[]{:S(2)}, u32[]{:S(2)}) collective-permute-start(f32[128,256]{1,0:T(8,128)S(1)} %slice_select_fusion.2), channel_id=1, source_target_pairs={{0,2},{1,3},{2,0},{3,1},{4,6},{5,7},{6,4},{7,5},{8,10},{9,11},{10,... | collective-permute-start | bytes 393224 | tf_op jit(solution)/shard_map/ppermute | solution.py:10
  60.2 5.0 %collective-permute-start.20 = (f32[128,256]{1,0:T(8,128)S(1)}, f32[128,256]{1,0:T(8,128)S(1)}, u32[]{:S(2)}, u32[]{:S(2)}) collective-permute-start(f32[128,256]{1,0:T(8,128)S(1)} %get-tuple-element.171), channel_id=1, source_target_pairs={{0,16},{16,0},{1,17},{17,1},{2,18},{18,2},{3,19},{19,3},{4,20},{20... | collective-permute-start | bytes 393224 | tf_op jit(solution)/shard_map/ppermute | solution.py:10
  61.8 0.9 %copy-start = (bf16[1,128,256]{2,1,0:T(8,128)(2,1)S(1)}, bf16[1,128,256]{2,1,0:T(8,128)(2,1)}, u32[]{:S(2)}) copy-start(bf16[1,128,256]{2,1,0:T(8,128)(2,1)} %param.6) | copy-start | bytes 196612
  65.2 5.9 %collective-permute-start.21 = (f32[128,256]{1,0:T(8,128)S(1)}, f32[128,256]{1,0:T(8,128)S(1)}, u32[]{:S(2)}, u32[]{:S(2)}) collective-permute-start(f32[128,256]{1,0:T(8,128)S(1)} %collective-permute-done.20), channel_id=1, source_target_pairs={{0,8},{1,9},{2,10},{3,11},{4,12},{5,13},{6,14},{7,15},{8,0},{9,1},... | collective-permute-start | bytes 393224 | tf_op jit(solution)/shard_map/ppermute | solution.py:10
where the time goes:
time: 72.1 us; the launch traced here: 71.9 us
  waiting for transfers between devices  30.6 us (42%)
  starting transfers between devices  29.9 us (41%)
  matrix products  6.37 us (9%)
  other arithmetic  2.87 us (4%)
  local copies, waits for them, and re-layouts  1.18 us (2%)
  between operations  0.78 us (1%)
    ppermute x22, waiting for transfers between devices, from_partner(): lax.ppermute(value, axis, [(i, i ^ 1 << bit) for i in range(lax.axis_size...  30.6 us
    ppermute x22, starting transfers between devices, from_partner(): lax.ppermute(value, axis, [(i, i ^ 1 << bit) for i in range(lax.axis_size...  29.9 us
    dot_general x8, matrix products, tile_scores(): jnp.einsum('ie,je->ij', row_tile, key_piece, preferred_element_type=jnp.f...  1.97 us
  transfers between devices with their start and end apart: 22, of which 14 were waited for; matrix products, arithmetic and copies ran while one was open for 3% of the time, Pallas kernels for 0%

commit v1 on v0

v1 whole, which is shorter than its diff:
```python
import functools
import math

import jax
import jax.numpy as jnp
from jax import lax
from jax.experimental import pallas as pl
from jax.experimental.pallas import tpu as pltpu
from jax.sharding import PartitionSpec as P

LOGIT_SCALE = 10.0
LOG2E = math.log2(math.e)
LN2 = math.log(2.0)
MESH = pl.DeviceIdType.MESH


def flip(value, mask):
    bit = 1
    while bit <= mask:
        if mask & bit:
            value = value + bit - 2 * bit * ((value // bit) % 2)
        bit *= 2
    return value


def kernel(views, devices, emb_ref, pos_ref, grad_ref, total_ref, loss_ref,
           own_ref, keys_ref, score_ref, total_send, total_all,
           own_sem, send_sem, direct_sem, cross_sem, core_sem, total_send_sem, total_sem):
    view = lax.axis_index("view")
    batch = lax.axis_index("batch")
    pair = lax.rem(view + views // 2, views)
    rows = own_ref.shape[0]
    lines = devices // 4

    sibling = flip(batch, 1)
    across = flip(batch, 2)

    def block(index):
        return keys_ref.at[pl.ds(pl.multiple_of(index * rows, rows), rows)]

    own_copy = pltpu.make_async_copy(emb_ref, own_ref, own_sem)
    own_copy.start()

    barrier = pltpu.get_barrier_semaphore()
    for step in range(devices):
        pl.semaphore_signal(barrier, inc=1, device_id=(pair, flip(batch, step)), device_id_type=MESH)
    pl.semaphore_signal(barrier, inc=1, device_id=(view, sibling), device_id_type=MESH)
    pl.semaphore_signal(barrier, inc=1, device_id=(view, across), device_id_type=MESH)
    pl.semaphore_wait(barrier, devices + 2)

    def direct(step):
        return pltpu.make_async_remote_copy(
            src_ref=emb_ref, dst_ref=block(batch), send_sem=send_sem, recv_sem=direct_sem.at[step],
            device_id=(pair, flip(batch, 4 * step)), device_id_type=MESH)

    def forward(index, target, sem):
        return pltpu.make_async_remote_copy(
            src_ref=block(index), dst_ref=block(index), send_sem=send_sem, recv_sem=sem,
            device_id=(view, target), device_id_type=MESH)

    for step in range(lines):
        direct(step).start()

    own_match = pos_ref[pl.ds(view, 1), :]
    far_match = pos_ref[pl.ds(pair, 1), :]
    lane_ids = lax.broadcasted_iota(jnp.int32, (rows, rows), 1)
    row_ids = lax.broadcasted_iota(jnp.int32, (rows, rows), 0)
    own_cols = jnp.broadcast_to(own_match.astype(jnp.float32), (rows, rows)).T
    own_hot = own_cols == lane_ids.astype(jnp.float32)
    far_hot = jnp.broadcast_to(far_match, (rows, rows)) == row_ids
    hot = (own_hot.astype(jnp.float32) + far_hot.astype(jnp.float32)).astype(jnp.bfloat16)
    own_copy.wait()

    def wait_on(index, sem):
        pltpu.make_async_remote_copy(
            src_ref=block(index), dst_ref=block(index), send_sem=send_sem, recv_sem=sem,
            device_id=(view, sibling), device_id_type=MESH).wait_recv()

    def take_direct(step):
        index = flip(batch, 4 * step)
        wait_on(index, direct_sem.at[step])
        forward(index, across, cross_sem.at[step]).start()
        forward(index, sibling, core_sem.at[2 * step]).start()

    def take_cross(step):
        index = flip(batch, 4 * step + 2)
        wait_on(index, cross_sem.at[step])
        forward(index, sibling, core_sem.at[2 * step + 1]).start()

    order = []

    def chunk_base(slot):
        step, side = slot // 2, slot % 2
        chip = flip(batch // 2, 2 * step + side)
        return chip

    def chunk(slot):
        return pl.ds(pl.multiple_of(chunk_base(slot) * (2 * rows), 2 * rows), 2 * rows)

    top = None

    def take_core(slot, top):
        step, side = slot // 2, slot % 2
        wait_on(flip(batch, 4 * step + 2 * side + 1), core_sem.at[slot])
        scores = lax.dot_general(own_ref[...], keys_ref[chunk(slot), :], (((1,), (1,)), ((), ())),
                                 preferred_element_type=jnp.float32) * (LOGIT_SCALE * LOG2E)
        score_ref[slot] = scores
        order.append(slot)
        return scores if top is None else jnp.maximum(top, scores)

    take_direct(0)
    for step in range(1, lines + 1):
        if step < lines:
            take_direct(step)
        take_cross(step - 1)
        top = take_core(2 * (step - 1), top)
        if step >= 2:
            top = take_core(2 * (step - 2) + 1, top)
        if step == 1:
            base = jnp.dot(hot, block(batch)[...], preferred_element_type=jnp.float32)
    top = take_core(2 * (lines - 1) + 1, top)

    row_max = jnp.max(top, axis=1, keepdims=True)
    summed = jnp.zeros((rows, 2 * rows), jnp.float32)
    for slot in order:
        summed = summed + jnp.exp2(score_ref[slot] - row_max)
    row_total = row_max + jnp.log(jnp.sum(summed, axis=1, keepdims=True)) * LOG2E

    first = score_ref[0]
    own_score = jnp.where(lax.rem(batch, 2) == 0, first[:, :rows], first[:, rows:])
    pos_score = jnp.sum(jnp.where(own_hot, own_score, 0.0), axis=1, keepdims=True)
    packed = jnp.where(lane_ids == 0, row_total, row_total - pos_score).T
    total_send[...] = packed[0:1, :]

    def send_total(step):
        return pltpu.make_async_remote_copy(
            src_ref=total_send, dst_ref=total_all.at[batch], send_sem=total_send_sem, recv_sem=total_sem,
            device_id=(pair, flip(batch, step)), device_id_type=MESH)

    for step in range(devices):
        send_total(step).start()
    total_ref[...] = packed[0:1, :] * LN2
    loss_ref[...] = packed[1:2, :] * LN2

    spread = -base
    for slot in order:
        weights = jnp.exp2(score_ref[slot] - row_total).astype(jnp.bfloat16)
        spread = spread + jnp.dot(weights, keys_ref[chunk(slot), :], preferred_element_type=jnp.float32)

    pltpu.make_async_remote_copy(
        src_ref=total_all, dst_ref=total_all, send_sem=total_send_sem, recv_sem=total_sem,
        device_id=(view, sibling), device_id_type=MESH).wait()
    for slot in order:
        chip = chunk_base(slot)
        far_total = jnp.concatenate([total_all[2 * chip], total_all[2 * chip + 1]], axis=1)
        weights = jnp.exp2(score_ref[slot] - far_total).astype(jnp.bfloat16)
        spread = spread + jnp.dot(weights, keys_ref[chunk(slot), :], preferred_element_type=jnp.float32)
    grad_ref[...] = spread * LOGIT_SCALE
    pltpu.make_async_remote_copy(
        src_ref=keys_ref, dst_ref=keys_ref, send_sem=send_sem, recv_sem=total_sem,
        device_id=(view, sibling), device_id_type=MESH).wait_send()


def body(views, devices, embeddings, positive):
    _, rows, width = embeddings.shape
    lines = devices // 4
    slots = devices // 2
    vmem = pl.BlockSpec(memory_space=pltpu.VMEM)
    grads, totals, losses = pl.pallas_call(
        functools.partial(kernel, views, devices),
        out_shape=(
            jax.ShapeDtypeStruct((rows, width), jnp.float32),
            jax.ShapeDtypeStruct((1, rows), jnp.float32),
            jax.ShapeDtypeStruct((1, rows), jnp.float32),
        ),
        in_specs=[pl.BlockSpec(memory_space=pl.ANY), vmem],
        out_specs=(vmem, vmem, vmem),
        scratch_shapes=[
            pltpu.VMEM((rows, width), jnp.bfloat16),
            pltpu.VMEM((devices * rows, width), jnp.bfloat16),
            pltpu.VMEM((slots, rows, 2 * rows), jnp.float32),
            pltpu.VMEM((1, rows), jnp.float32),
            pltpu.VMEM((devices, 1, rows), jnp.float32),
            pltpu.SemaphoreType.DMA,
            pltpu.SemaphoreType.DMA,
            pltpu.SemaphoreType.DMA((lines,)),
            pltpu.SemaphoreType.DMA((lines,)),
            pltpu.SemaphoreType.DMA((slots,)),
            pltpu.SemaphoreType.DMA,
            pltpu.SemaphoreType.DMA,
        ],
        compiler_params=pltpu.CompilerParams(
            collective_id=0, has_side_effects=True, vmem_limit_bytes=32 * 1024 * 1024),
    )(embeddings.reshape(rows, width), positive)
    return grads[None], totals, losses


def solution(mesh):
    return jax.shard_map(
        functools.partial(body, mesh.shape["view"], mesh.shape["batch"]),
        mesh=mesh,
        in_specs=(P("view", "batch", None), P(None, "batch")),
        out_specs=(P("view", "batch", None), P("view", "batch"), P("view", "batch")),
        check_vma=False,
    )
```

time: 72.1 us -> 31.7 us (0.44)
  waiting for transfers between devices: 30.6 us -> 0 us
  starting transfers between devices: 29.9 us -> 0 us
  Pallas kernels: 0 us -> 27.7 us
  matrix products: 6.37 us -> 0 us
  other arithmetic: 2.87 us -> 0 us
  local copies, waits for them, and re-layouts: 1.18 us -> 3.19 us
    ppermute x22 -> x0, waiting for transfers between devices: 30.6 us -> none  [from_partner(): lax.ppermute(value, axis, [(i, i ^ 1 << bit) for i in range(lax.axis_size...]
    ppermute x22 -> x0, starting transfers between devices: 29.9 us -> none  [from_partner(): lax.ppermute(value, axis, [(i, i ^ 1 << bit) for i in range(lax.axis_size...]
    pallas_call x0 -> x1, Pallas kernels: none -> 27.7 us  [body(): pl.pallas_call(functools.partial(kernel, views, devices), out_shape=(jax....]
    dot_general x25 -> x0, matrix products: 6.37 us -> none  [the longest x8 1.97 us: tile_scores(): jnp.einsum('ie,je->ij', row_tile, key_piece, preferred_element_type=jnp.f...]
    unnamed x4 -> x7, local copies, waits for them, and re-layouts: 0.01 us -> 3.19 us
    select_n x9 -> x0, other arithmetic: 1.15 us -> none  [the longest x1 0.85 us: tile_terms(): row_tile = jnp.where(is_key, flipped, own_rows)]
    reduce_sum x5 -> x0, other arithmetic: 0.94 us -> none  [the longest x4 0.76 us: stat_step(): column_sum = jnp.sum(jnp.exp(scores - column_max[None, :]), axis=0)]
    gather x1 -> x0, local copies, waits for them, and re-layouts: 0.85 us -> none  [body(): pos_rows = jnp.take(partner, own_match, axis=0).astype(jnp.float32)]
  transfers between devices with their start and end apart: 22 -> 0, of which waited for: 14 -> 0; matrix products, arithmetic and copies ran while one was open for 3% -> 0% of each run, Pallas kernels for 0% -> 0%
where the time goes in v1:
time: 31.7 us; the launch traced here: 31.5 us
  Pallas kernels  27.7 us (87%)
  local copies, waits for them, and re-layouts  3.19 us (10%)
  between operations  0.65 us (2%)
    pallas_call x1, Pallas kernels, body(): pl.pallas_call(functools.partial(kernel, views, devices), out_shape=(jax....  27.7 us
    unnamed x7, local copies, waits for them, and re-layouts  3.19 us

profile of v1, /device:TPU:0, one launch (start us, length us, event | category | flops | bytes accessed | tf_op | source)
XLA Modules:
  0.0 31.5 jit_solution(8107057051780564859)
XLA Ops:
  0.6 0.0 copy-start.1
  0.6 0.7 %copy-done.1 = s32[2,128]{1,0:T(2,128)S(1)} copy-done((s32[2,128]{1,0:T(2,128)S(1)}, s32[2,128]{1,0:T(2,128)}, u32[]{:S(2)}) %copy-start.1) | copy-done | bytes 1048
  1.3 0.0 copy-start
  1.3 0.8 %copy-done = bf16[1,128,256]{2,1,0:T(8,128)(2,1)S(1)} copy-done((bf16[1,128,256]{2,1,0:T(8,128)(2,1)S(1)}, bf16[1,128,256]{2,1,0:T(8,128)(2,1)}, u32[]{:S(2)}) %copy-start) | copy-done | bytes 65560
  2.1 27.7 %shard_map.49 = (f32[128,256]{1,0:T(8,128)S(1)}, f32[1,128]{1,0:T(1,128)S(1)}, f32[1,128]{1,0:T(1,128)S(1)}) custom-call(bf16[128,256]{1,0:T(8,128)(2,1)S(1)} %bitcast.3, s32[2,128]{1,0:T(2,128)S(1)} %copy-done.1), custom_call_target="tpu_custom_call" | custom-call | tf_op jit(solution)/shard_map/pallas_call | solution.py:169
  29.9 0.7 %copy.8 = f32[1,128,256]{2,1,0:T(8,128)} copy(f32[1,128,256]{2,1,0:T(8,128)S(1)} %bitcast.2) | data formatting | bytes 262144
  30.5 0.5 %copy.9 = f32[1,128]{1,0:T(1,128)} copy(f32[1,128]{1,0:T(1,128)S(1)} %get-tuple-element.13) | data formatting | bytes 1024
  31.0 0.5 %copy.10 = f32[1,128]{1,0:T(1,128)} copy(f32[1,128]{1,0:T(1,128)S(1)} %get-tuple-element.14) | data formatting | bytes 1024
Async XLA Ops:
  0.6 0.7 %copy-start.1 = (s32[2,128]{1,0:T(2,128)S(1)}, s32[2,128]{1,0:T(2,128)}, u32[]{:S(2)}) copy-start(s32[2,128]{1,0:T(2,128)} %pos_ref.1) | copy-start | bytes 3076
  1.3 0.8 %copy-start = (bf16[1,128,256]{2,1,0:T(8,128)(2,1)S(1)}, bf16[1,128,256]{2,1,0:T(8,128)(2,1)}, u32[]{:S(2)}) copy-start(bf16[1,128,256]{2,1,0:T(8,128)(2,1)} %param.2) | copy-start | bytes 196612

commit v2 on v1

v2 whole, which is shorter than its diff:
```python
import functools
import math

import jax
import jax.numpy as jnp
from jax import lax
from jax.experimental import pallas as pl
from jax.experimental.pallas import tpu as pltpu
from jax.sharding import PartitionSpec as P

LOGIT_SCALE = 10.0
LOG2E = math.log2(math.e)
LN2 = math.log(2.0)
MESH = pl.DeviceIdType.MESH


def flip(value, mask):
    bit = 1
    while bit <= mask:
        if mask & bit:
            value = value + bit - 2 * bit * ((value // bit) % 2)
        bit *= 2
    return value


def merge(first, second):
    top = jnp.maximum(first, second)
    return top + jnp.log(jnp.exp2(first - top) + jnp.exp2(second - top)) * LOG2E


def kernel(views, devices, emb_ref, pos_hbm, grad_ref, total_ref, loss_ref,
           own_ref, pos_ref, keys_ref, score_ref, weight_ref, part_send, part_near, part_far, grad_send, grad_near,
           local_sem, send_sem, near_send_sem, near_sem, direct_sem, core_sem, far_send_sem, far_sem):
    view = lax.axis_index("view")
    batch = lax.axis_index("batch")
    pair = lax.rem(view + views // 2, views)
    rows = own_ref.shape[0] // 2
    lines = devices // 4
    line = batch // 4
    core = lax.rem(batch, 2)
    sibling = flip(batch, 1)
    across = flip(batch, 2)

    own_copy = pltpu.make_async_copy(emb_ref, own_ref.at[pl.ds(0, rows)], local_sem.at[0])
    own_copy.start()
    pos_copy = pltpu.make_async_copy(pos_hbm, pos_ref, local_sem.at[1])
    pos_copy.start()

    barrier = pltpu.get_barrier_semaphore()
    for step in reversed(range(devices)):
        pl.semaphore_signal(barrier, inc=1, device_id=(pair, flip(batch, step)), device_id_type=MESH)
    pl.semaphore_signal(barrier, inc=1, device_id=(view, across), device_id_type=MESH)
    pl.semaphore_signal(barrier, inc=1, device_id=(view, sibling), device_id_type=MESH)

    own_copy.wait()
    pos_copy.wait()
    own_match = pos_ref[pl.ds(view, 1), :]
    far_match = pos_ref[pl.ds(pair, 1), :]
    lane_ids = lax.broadcasted_iota(jnp.int32, (rows, rows), 1)
    row_ids = lax.broadcasted_iota(jnp.int32, (rows, rows), 0)
    own_cols = jnp.broadcast_to(own_match.astype(jnp.float32), (rows, rows)).T
    own_hot = own_cols == lane_ids.astype(jnp.float32)
    far_hot = jnp.broadcast_to(far_match, (rows, rows)) == row_ids
    hot = (own_hot.astype(jnp.float32) + far_hot.astype(jnp.float32)).astype(jnp.bfloat16)

    pl.semaphore_wait(barrier, devices + 2)

    def block(chain, side):
        return keys_ref.at[pl.ds(pl.multiple_of((2 * chain + side) * rows, rows), rows)]

    def near(src, dst, index):
        return pltpu.make_async_remote_copy(
            src_ref=src, dst_ref=dst, send_sem=near_send_sem.at[index], recv_sem=near_sem.at[index],
            device_id=(view, across), device_id_type=MESH)

    def direct(step):
        return pltpu.make_async_remote_copy(
            src_ref=emb_ref, dst_ref=block(line, core), send_sem=send_sem, recv_sem=direct_sem.at[step],
            device_id=(pair, flip(batch, 4 * step)), device_id_type=MESH)

    def to_sibling(chain, side, sem):
        return pltpu.make_async_remote_copy(
            src_ref=block(chain, side), dst_ref=block(chain, side), send_sem=send_sem, recv_sem=sem,
            device_id=(view, sibling), device_id_type=MESH)

    anchors_copy = near(emb_ref, own_ref.at[pl.ds(rows, rows)], 0)
    for step in range(lines):
        direct(step).start()
    anchors_copy.start()

    def take_direct(step):
        chain = flip(line, step)
        to_sibling(chain, core, direct_sem.at[step]).wait_recv()
        to_sibling(chain, core, core_sem.at[step]).start()

    def chunk(step):
        return keys_ref[pl.ds(pl.multiple_of(flip(line, step) * (2 * rows), 2 * rows), 2 * rows), :]

    def take_core(step, top):
        to_sibling(flip(line, step), 1 - core, core_sem.at[step]).wait_recv()
        scores = lax.dot_general(own_ref[...], chunk(step), (((1,), (1,)), ((), ())),
                                 preferred_element_type=jnp.float32) * (LOGIT_SCALE * LOG2E)
        score_ref[step] = scores
        return scores if top is None else jnp.maximum(top, scores)

    top = None
    for step in range(lines):
        take_direct(step)
        if step == 0:
            base = jnp.dot(hot, block(line, core)[...], preferred_element_type=jnp.float32)
            anchors_copy.wait_recv()
        if step >= 1:
            top = take_core(step - 1, top)
    top = take_core(lines - 1, top)

    row_max = jnp.max(top, axis=1, keepdims=True)
    summed = jnp.zeros((2 * rows, 2 * rows), jnp.float32)
    for step in range(lines):
        summed = summed + jnp.exp2(score_ref[step] - row_max)
    row_part = row_max + jnp.log(jnp.sum(summed, axis=1, keepdims=True)) * LOG2E

    first = score_ref[0, :rows, :]
    own_score = jnp.where(core == 0, first[:, :rows], first[:, rows:])
    pos_score = jnp.sum(jnp.where(own_hot, own_score, 0.0), axis=1, keepdims=True)
    packed = jnp.where(lane_ids == 0, row_part[:rows], jnp.where(lane_ids == 1, row_part[rows:], pos_score)).T
    part_send[0] = packed[0:1, :]
    part_send[1] = packed[1:2, :]

    near_copy = near(part_send, part_near, 1)
    near_copy.start()
    for step in reversed(range(devices)):
        pltpu.make_async_remote_copy(
            src_ref=part_send.at[(step // 2) % 2], dst_ref=part_far.at[batch],
            send_sem=far_send_sem, recv_sem=far_sem,
            device_id=(pair, flip(batch, step)), device_id_type=MESH).start()

    near_copy.wait_recv()
    own_total = merge(packed[0:1, :], part_near[1])
    across_total = merge(packed[1:2, :], part_near[0])
    total_ref[...] = own_total * LN2
    loss_ref[...] = (own_total - packed[2:3, :]) * LN2

    def column(values):
        tall = jnp.broadcast_to(values, (rows, rows)).T
        return jnp.concatenate([tall, tall], axis=1)

    for half, values in enumerate((own_total, across_total)):
        tall = column(values)
        for step in range(lines):
            weight_ref[step, half * rows:(half + 1) * rows, :] = jnp.exp2(
                score_ref[step, half * rows:(half + 1) * rows, :] - tall)

    pltpu.make_async_remote_copy(
        src_ref=part_far, dst_ref=part_far, send_sem=far_send_sem, recv_sem=far_sem,
        device_id=(view, sibling), device_id_type=MESH).wait()

    def far_total(step):
        start = 4 * flip(line, step)
        return jnp.concatenate(
            [merge(part_far[start + side], part_far[start + 2 + side]) for side in range(2)], axis=1)

    far_totals = [far_total(step) for step in range(lines)]

    def spread(half, result):
        for step in range(lines):
            span = slice(half * rows, (half + 1) * rows)
            weights = weight_ref[step, span, :] + jnp.exp2(score_ref[step, span, :] - far_totals[step])
            part = jnp.dot(weights.astype(jnp.bfloat16), chunk(step), preferred_element_type=jnp.float32)
            result = part if result is None else result + part
        return result

    grad_send[...] = spread(1, None)
    grad_copy = near(grad_send, grad_near, 2)
    grad_copy.start()
    own_spread = spread(0, -base)
    anchors_copy.wait_send()
    near_copy.wait_send()
    pltpu.make_async_remote_copy(
        src_ref=keys_ref, dst_ref=keys_ref, send_sem=send_sem, recv_sem=far_sem,
        device_id=(view, sibling), device_id_type=MESH).wait_send()
    grad_copy.wait_recv()
    grad_ref[...] = (own_spread + grad_near[...]) * LOGIT_SCALE
    grad_copy.wait_send()


def body(views, devices, embeddings, positive):
    _, rows, width = embeddings.shape
    lines = devices // 4
    vmem = pl.BlockSpec(memory_space=pltpu.VMEM)
    hbm = pl.BlockSpec(memory_space=pltpu.HBM)
    dma = pltpu.SemaphoreType.DMA
    grads, totals, losses = pl.pallas_call(
        functools.partial(kernel, views, devices),
        out_shape=(
            jax.ShapeDtypeStruct((rows, width), jnp.float32),
            jax.ShapeDtypeStruct((1, rows), jnp.float32),
            jax.ShapeDtypeStruct((1, rows), jnp.float32),
        ),
        in_specs=[hbm, hbm],
        out_specs=(vmem, vmem, vmem),
        scratch_shapes=[
            pltpu.VMEM((2 * rows, width), jnp.bfloat16),
            pltpu.VMEM(positive.shape, jnp.int32),
            pltpu.VMEM((2 * lines * rows, width), jnp.bfloat16),
            pltpu.VMEM((lines, 2 * rows, 2 * rows), jnp.float32),
            pltpu.VMEM((lines, 2 * rows, 2 * rows), jnp.float32),
            pltpu.VMEM((2, 1, rows), jnp.float32),
            pltpu.VMEM((2, 1, rows), jnp.float32),
            pltpu.VMEM((devices, 1, rows), jnp.float32),
            pltpu.VMEM((rows, width), jnp.float32),
            pltpu.VMEM((rows, width), jnp.float32),
            dma((2,)), dma, dma((3,)), dma((3,)), dma((lines,)), dma((lines,)), dma, dma,
        ],
        compiler_params=pltpu.CompilerParams(
            collective_id=0, has_side_effects=True, vmem_limit_bytes=60 * 1024 * 1024),
    )(embeddings.reshape(rows, width), positive)
    return grads[None], totals, losses


def solution(mesh):
    return jax.shard_map(
        functools.partial(body, mesh.shape["view"], mesh.shape["batch"]),
        mesh=mesh,
        in_specs=(P("view", "batch", None), P(None, "batch")),
        out_specs=(P("view", "batch", None), P("view", "batch"), P("view", "batch")),
        check_vma=False,
    )
```

time: 31.7 us -> 30.1 us (0.950)
  Pallas kernels: 27.7 us -> 26.5 us
  local copies, waits for them, and re-layouts: 3.19 us -> 2.75 us
    pallas_call x1, Pallas kernels: 27.7 us -> 26.5 us  [body(): pl.pallas_call(functools.partial(kernel, views, devices), out_shape=(jax....]
    unnamed x7, local copies, waits for them, and re-layouts: 3.19 us -> 2.75 us
where the time goes in v2:
time: 30.1 us; the launch traced here: 29.9 us
  Pallas kernels  26.5 us (88%)
  local copies, waits for them, and re-layouts  2.75 us (9%)
  between operations  0.65 us (2%)
    pallas_call x1, Pallas kernels, body(): pl.pallas_call(functools.partial(kernel, views, devices), out_shape=(jax....  26.5 us
    unnamed x7, local copies, waits for them, and re-layouts  2.75 us

profile of v2, /device:TPU:0, one launch (start us, length us, event | category | flops | bytes accessed | tf_op | source)
XLA Modules:
  0.0 29.9 jit_solution(5092848993065574414)
XLA Ops:
  0.6 26.5 %shard_map.49 = (f32[128,256]{1,0:T(8,128)}, f32[1,128]{1,0:T(1,128)}, f32[1,128]{1,0:T(1,128)}) custom-call(bf16[128,256]{1,0:T(8,128)(2,1)} %bitcast.3, s32[2,128]{1,0:T(2,128)} %pos_hbm.1), custom_call_target="tpu_custom_call" | custom-call | tf_op jit(solution)/shard_map/pallas_call | solution.py:192
  27.1 0.0 copy-start.1
  27.1 1.6 %copy.8 = f32[1,128,256]{2,1,0:T(8,128)} copy(f32[1,128,256]{2,1,0:T(8,128)} %bitcast.2) | data formatting | bytes 262144
  28.7 0.0 copy-done.1
  28.7 0.0 copy-start
  28.7 0.5 %copy.9 = f32[1,128]{1,0:T(1,128)} copy(f32[1,128]{1,0:T(1,128)S(1)} %copy-done.1) | data formatting | bytes 1024
  29.2 0.2 copy-done
  29.4 0.5 %copy.10 = f32[1,128]{1,0:T(1,128)} copy(f32[1,128]{1,0:T(1,128)S(1)} %copy-done) | data formatting | bytes 1024
Async XLA Ops:
  27.1 1.6 %copy-start.1 = (f32[1,128]{1,0:T(1,128)S(1)}, f32[1,128]{1,0:T(1,128)}, u32[]{:S(2)}) copy-start(f32[1,128]{1,0:T(1,128)} %get-tuple-element.13) | copy-start | bytes 1540
  28.7 0.7 %copy-start = (f32[1,128]{1,0:T(1,128)S(1)}, f32[1,128]{1,0:T(1,128)}, u32[]{:S(2)}) copy-start(f32[1,128]{1,0:T(1,128)} %get-tuple-element.14) | copy-start | bytes 1540

commit v3 on v2

--- a/solution.py
+++ b/solution.py
@@ -28,7 +28,7 @@
     return top + jnp.log(jnp.exp2(first - top) + jnp.exp2(second - top)) * LOG2E
 
 
-def kernel(views, devices, emb_ref, pos_hbm, grad_ref, total_ref, loss_ref,
+def kernel(views, devices, emb_ref, pos_hbm, grad_ref, stats_ref,
            own_ref, pos_ref, keys_ref, score_ref, weight_ref, part_send, part_near, part_far, grad_send, grad_near,
            local_sem, send_sem, near_send_sem, near_sem, direct_sem, core_sem, far_send_sem, far_sem):
     view = lax.axis_index("view")
@@ -137,8 +137,8 @@
     near_copy.wait_recv()
     own_total = merge(packed[0:1, :], part_near[1])
     across_total = merge(packed[1:2, :], part_near[0])
-    total_ref[...] = own_total * LN2
-    loss_ref[...] = (own_total - packed[2:3, :]) * LN2
+    stats_ref[0:1, :] = own_total
+    stats_ref[1:2, :] = own_total - packed[2:3, :]
 
     def column(values):
         tall = jnp.broadcast_to(values, (rows, rows)).T
@@ -169,7 +169,7 @@
             result = part if result is None else result + part
         return result
 
-    grad_send[...] = spread(1, None)
+    grad_send[...] = spread(1, None).astype(grad_send.dtype)
     grad_copy = near(grad_send, grad_near, 2)
     grad_copy.start()
     own_spread = spread(0, -base)
@@ -179,8 +179,14 @@
         src_ref=keys_ref, dst_ref=keys_ref, send_sem=send_sem, recv_sem=far_sem,
         device_id=(view, sibling), device_id_type=MESH).wait_send()
     grad_copy.wait_recv()
-    grad_ref[...] = (own_spread + grad_near[...]) * LOGIT_SCALE
+    grad_ref[...] = own_spread + grad_near[...].astype(jnp.float32)
     grad_copy.wait_send()
+
+
+def finish(spread_ref, stats_ref, grad_ref, total_ref, loss_ref):
+    grad_ref[...] = spread_ref[...] * LOGIT_SCALE
+    total_ref[...] = stats_ref[0:1, :] * LN2
+    loss_ref[...] = stats_ref[1:2, :] * LN2
 
 
 def body(views, devices, embeddings, positive):
@@ -189,15 +195,14 @@
     vmem = pl.BlockSpec(memory_space=pltpu.VMEM)
     hbm = pl.BlockSpec(memory_space=pltpu.HBM)
     dma = pltpu.SemaphoreType.DMA
-    grads, totals, losses = pl.pallas_call(
+    spread, stats = pl.pallas_call(
         functools.partial(kernel, views, devices),
         out_shape=(
             jax.ShapeDtypeStruct((rows, width), jnp.float32),
-            jax.ShapeDtypeStruct((1, rows), jnp.float32),
-            jax.ShapeDtypeStruct((1, rows), jnp.float32),
+            jax.ShapeDtypeStruct((2, rows), jnp.float32),
         ),
         in_specs=[hbm, hbm],
-        out_specs=(vmem, vmem, vmem),
+        out_specs=(vmem, vmem),
         scratch_shapes=[
             pltpu.VMEM((2 * rows, width), jnp.bfloat16),
             pltpu.VMEM(positive.shape, jnp.int32),
@@ -207,13 +212,23 @@
             pltpu.VMEM((2, 1, rows), jnp.float32),
             pltpu.VMEM((2, 1, rows), jnp.float32),
             pltpu.VMEM((devices, 1, rows), jnp.float32),
-            pltpu.VMEM((rows, width), jnp.float32),
-            pltpu.VMEM((rows, width), jnp.float32),
+            pltpu.VMEM((rows, width), jnp.bfloat16),
+            pltpu.VMEM((rows, width), jnp.bfloat16),
             dma((2,)), dma, dma((3,)), dma((3,)), dma((lines,)), dma((lines,)), dma, dma,
         ],
         compiler_params=pltpu.CompilerParams(
             collective_id=0, has_side_effects=True, vmem_limit_bytes=60 * 1024 * 1024),
     )(embeddings.reshape(rows, width), positive)
+    grads, totals, losses = pl.pallas_call(
+        finish,
+        out_shape=(
+            jax.ShapeDtypeStruct((rows, width), jnp.float32),
+            jax.ShapeDtypeStruct((1, rows), jnp.float32),
+            jax.ShapeDtypeStruct((1, rows), jnp.float32),
+        ),
+        in_specs=[vmem, vmem],
+        out_specs=(vmem, vmem, vmem),
+    )(spread, stats)
     return grads[None], totals, losses
 
 

time: 30.1 us -> 27.6 us (0.917)
  local copies, waits for them, and re-layouts: 2.75 us -> 0 us
    unnamed x7 -> x0, local copies, waits for them, and re-layouts: 2.75 us -> none
    pallas_call x0 -> x1, Pallas kernels: none -> 1.58 us  [body(): pl.pallas_call(finish, out_shape=(jax.ShapeDtypeStruct((rows, width), jnp...]
    pallas_call x1, Pallas kernels: 26.5 us -> 25.3 us  [body(): pl.pallas_call(functools.partial(kernel, views, devices), out_shape=(jax....]
where the time goes in v3:
time: 27.6 us; the launch traced here: 27.5 us
  Pallas kernels  26.8 us (97%)
  between operations  0.64 us (2%)
    pallas_call x1, Pallas kernels, body(): pl.pallas_call(functools.partial(kernel, views, devices), out_shape=(jax....  25.3 us
    pallas_call x1, Pallas kernels, body(): pl.pallas_call(finish, out_shape=(jax.ShapeDtypeStruct((rows, width), jnp...  1.58 us

profile of v3, /device:TPU:0, one launch (start us, length us, event | category | flops | bytes accessed | tf_op | source)
XLA Modules:
  0.0 27.5 jit_solution(17171061151616718318)
XLA Ops:
  0.6 25.3 %shard_map.49 = (f32[128,256]{1,0:T(8,128)}, f32[2,128]{1,0:T(2,128)}) custom-call(bf16[128,256]{1,0:T(8,128)(2,1)} %bitcast.2, s32[2,128]{1,0:T(2,128)} %pos_hbm.1), custom_call_target="tpu_custom_call" | custom-call | tf_op jit(solution)/shard_map/pallas_call | solution.py:198
  25.9 1.6 %shard_map.50 = (f32[128,256]{1,0:T(8,128)}, f32[1,128]{1,0:T(1,128)}, f32[1,128]{1,0:T(1,128)}) custom-call(f32[128,256]{1,0:T(8,128)} %get-tuple-element.8.spread_ref, f32[2,128]{1,0:T(2,128)} %get-tuple-element.9.stats_ref), custom_call_target="tpu_custom_call" | custom-call | tf_op jit(solution)/shard_map/pallas_call | solution.py:222
